TPU v7x, 128 devices: a whole 4x4x4 slice. The times are simulated.
128 devices in a mesh: row: 4 (over z), col: 8 (over x_hi, y), tp: 4 (over x_lo, core).
Axes of the slice: x: 4 (x_hi: 2, x_lo: 2; x = x_hi * 2 + x_lo), y: 4, z: 4, core: 2. Of those that a mesh axis runs over, the one named last changes fastest.
Arguments:
- tokens: bfloat16 [32, 128, 3200], P('row', 'col', 'tp'), may hold values from -6 to 6
- cotangent: bfloat16 [32, 128, 3200], P('row', 'col', 'tp'), may hold values from -6 to 6
- expand_weight: bfloat16 [3200, 6400], P(None, 'tp'), may hold values from -0.10606602 to 0.10606602
- reduce_weight: bfloat16 [3200, 6400], P(None, 'tp'), may hold values from -0.075 to 0.075
- position_kernel: float32 [3, 3, 3200], replicated, may hold values from -1.5 to 1.5
- norm_gain: float32 [3200], replicated, may hold values from 0.2 to 2.4
Outputs:
- grad_tokens: bfloat16 [32, 128, 3200], P('row', 'col', 'tp')
- grad_expand: float32 [3200, 6400], P(('row', 'col'), 'tp')
- grad_reduce: float32 [3200, 6400], P(('row', 'col'), 'tp')
- grad_kernel: float32 [3, 3, 3200], P(None, None, 'tp')
- grad_gain: float32 [3200], P('tp')
All inputs are finite; a program needn't handle non-finite values.
Results may differ from a plain program's by a relative error of at most 0.029.
Values may be sent and summed in bfloat16 or wider, within the bound.
A program may use at most 192 MiB of HBM per device.

v0:
```python
import jax
import jax.numpy as jnp
from jax import lax
from jax.sharding import PartitionSpec as P

epsilon = 1e-06


def padded_2(cells, sides, width):
    for axis, dim in sides:
        count = lax.axis_size(axis)
        ends = count - 1
        head = lax.slice_in_dim(cells, 0, width, axis=dim)
        tail = lax.slice_in_dim(cells, cells.shape[dim] - width, cells.shape[dim], axis=dim)
        cells = jnp.concatenate(
            [
                lax.ppermute(tail, axis, [(i, (i + 1) % count) for i in range(ends)]),
                cells,
                lax.ppermute(head, axis, [((i + 1) % count, i) for i in range(ends)]),
            ],
            axis=dim,
        )
    return cells


def conv_forward(padded, kernel, row_cells, col_cells):
    summed = jnp.zeros((row_cells, col_cells, padded.shape[2]), jnp.float32)
    for row_shift in range(3):
        for col_shift in range(3):
            summed = (
                summed
                + kernel[row_shift, col_shift]
                * padded[row_shift : row_shift + row_cells, col_shift : col_shift + col_cells]
            )
    return summed


def conv_back(padded, kernel, row_cells, col_cells):
    summed = jnp.zeros((row_cells, col_cells, padded.shape[2]), jnp.float32)
    for row_shift in range(3):
        for col_shift in range(3):
            summed = (
                summed
                + kernel[row_shift, col_shift]
                * padded[
                    2 - row_shift : 2 - row_shift + row_cells,
                    2 - col_shift : 2 - col_shift + col_cells,
                ]
            )
    return summed


def kernel_terms(grad_field, padded, row_cells, col_cells):
    pieces = []
    for row_shift in range(3):
        for col_shift in range(3):
            pieces.append(
                jnp.sum(
                    grad_field
                    * padded[row_shift : row_shift + row_cells, col_shift : col_shift + col_cells],
                    axis=(0, 1),
                )
            )
    return jnp.stack(pieces).reshape(3, 3, grad_field.shape[2])


def gelu_slope(pre_act):
    cdf = 0.5 * (1.0 + lax.erf(pre_act * 0.7071067811865476))
    density = jnp.exp(-0.5 * pre_act * pre_act) * 0.3989422804014327
    return cdf + pre_act * density


def on_device(tokens, cotangent, expand_weight, reduce_weight, position_kernel, norm_gain):
    row_cells, col_cells, quarter = tokens.shape
    feature_width = quarter * lax.axis_size("tp")
    offset = lax.axis_index("tp") * quarter
    grid_devices = lax.axis_size("row") * lax.axis_size("col")
    factor = float(row_cells * col_cells * grid_devices) ** (-0.5)
    own_kernel = lax.dynamic_slice_in_dim(position_kernel, offset, quarter, 2)
    own_gain = lax.dynamic_slice_in_dim(norm_gain, offset, quarter, 0)
    padded_x = padded_2(tokens, (("row", 0), ("col", 1)), 1)
    own_h = (
        tokens.astype(jnp.float32)
        + conv_forward(padded_x.astype(jnp.float32), own_kernel, row_cells, col_cells)
    ).astype(jnp.bfloat16)
    whole_h, full_cot = (
        lax.all_gather(own_h, "tp", axis=2, tiled=True),
        lax.all_gather(cotangent, "tp", axis=2, tiled=True),
    )
    flat_cot = full_cot.reshape(row_cells * col_cells, feature_width)
    d_act = jnp.dot(flat_cot, reduce_weight, preferred_element_type=jnp.float32)
    h_float = whole_h.astype(jnp.float32)
    inverse = lax.rsqrt(jnp.mean(h_float * h_float, axis=-1, keepdims=True) + epsilon)
    normed = (
        (h_float * inverse * norm_gain)
        .astype(jnp.bfloat16)
        .reshape(row_cells * col_cells, feature_width)
    )
    pre_act = jnp.dot(normed, expand_weight, preferred_element_type=jnp.float32)
    activated = jax.nn.gelu(pre_act, approximate=False).astype(jnp.bfloat16)
    d_pre = (d_act * gelu_slope(pre_act)).astype(jnp.bfloat16)
    hidden_part = expand_weight.shape[1]
    d_norm = lax.dot_general(
        d_pre, expand_weight, (((1,), (1,)), ((), ())), preferred_element_type=jnp.float32
    )
    d_norm = d_norm.reshape(row_cells, col_cells, feature_width)
    own_hf = own_h.astype(jnp.float32)
    own_dn = lax.psum_scatter(
        d_norm.astype(jnp.bfloat16), "tp", scatter_dimension=2, tiled=True
    ).astype(jnp.float32)
    inner_dot = lax.psum(jnp.sum(own_dn * own_gain * own_hf, axis=-1, keepdims=True), "tp")
    scaled = own_dn * own_gain
    d_mlp = inverse * scaled - own_hf * inverse**3 * inner_dot / feature_width
    d_hidden = (cotangent.astype(jnp.float32) + d_mlp).astype(jnp.bfloat16)
    padded_dh = padded_2(d_hidden, (("row", 0), ("col", 1)), 1)
    dh_float = d_hidden.astype(jnp.float32)
    grad_tokens = (
        dh_float + conv_back(padded_dh.astype(jnp.float32), own_kernel, row_cells, col_cells)
    ).astype(jnp.bfloat16)
    both_grads = lax.psum_scatter(
        jnp.concatenate(
            [
                lax.dot_general(
                    normed, d_pre, (((0,), (0,)), ((), ())), preferred_element_type=jnp.float32
                )
                * factor,
                lax.dot_general(
                    flat_cot,
                    activated,
                    (((0,), (0,)), ((), ())),
                    preferred_element_type=jnp.float32,
                )
                * factor,
            ],
            axis=1,
        ).astype(jnp.bfloat16),
        ("row", "col"),
        scatter_dimension=0,
        tiled=True,
    ).astype(jnp.float32)
    grad_expand = both_grads[:, :hidden_part]
    grad_reduce = both_grads[:, hidden_part:]
    local_gain = jnp.sum(own_dn * own_hf * inverse, axis=(0, 1)) * factor
    local_kernel = (
        kernel_terms(dh_float, padded_x.astype(jnp.float32), row_cells, col_cells) * factor
    )
    grad_gain, grad_kernel = lax.psum((local_gain, local_kernel), ("row", "col"))
    return (grad_tokens, grad_expand, grad_reduce, grad_kernel, grad_gain)


def solution(mesh):
    placed = (P("row", "col", "tp"), P("row", "col", "tp"), P(None, "tp"), P(None, "tp"), P(), P())
    return jax.shard_map(
        on_device,
        mesh=mesh,
        in_specs=placed,
        out_specs=(
            P("row", "col", "tp"),
            P(("row", "col"), "tp"),
            P(("row", "col"), "tp"),
            P(None, None, "tp"),
            P("tp"),
        ),
        check_vma=False,
    )
```

profile of v0, /device:TPU:0, one launch (start us, length us, event | category | flops | bytes accessed | tf_op | source)
XLA Modules:
  0.0 673.6 jit_solution(9972905049139235258)
XLA Ops:
  8.0 0.0 reduce-scatter.5.cloned.1.call-start
  8.1 0.8 fusion.111
  8.9 3.9 collective-permute-start
  12.8 1.3 collective-permute-start.1
  14.1 2.9 copy.81
  17.0 1.0 constant_dynamic-update-slice_fusion.1
  17.9 0.6 collective-permute-done.1
  18.6 0.1 fusion.109
  18.6 1.3 collective-permute-start.3
  19.9 4.5 collective-permute-start.2
  24.5 40.4 %all_gather.7 = bf16[8,16,3200]{1,0,2:T(8,128)(2,1)} all-gather(bf16[8,16,800]{1,0,2:T(8,128)(2,1)S(1)} %copy.81), channel_id=1, replica_groups=mesh['row'=4,'col'=8,'tp'=4] {'tp'}, dimensions={2}, use_global_device_ids=true | all-gather | bytes 1024000 | tf_op jit(solution)/shard_map/all_gather | solution.py:88
  64.9 6.1 copy.82
  71.0 1.0 dynamic-slice_reduce_fusion.8
  72.2 0.2 maximum_convert_fusion
  72.4 0.2 copy-done.5
  72.6 0.0 copy-done.7
  72.7 0.0 copy-done.9
  72.7 0.0 copy-done.11
  72.7 0.0 copy-done.13
  72.7 0.0 copy-done.15
  72.7 0.0 copy-done.17
  72.7 0.4 add_convert_fusion
  73.1 2.0 copy.79
  75.1 40.8 %all_gather.6 = bf16[8,16,3200]{1,0,2:T(8,128)(2,1)} all-gather(bf16[8,16,800]{1,0,2:T(8,128)(2,1)S(1)} %copy.79), channel_id=1, replica_groups=mesh['row'=4,'col'=8,'tp'=4] {'tp'}, dimensions={2}, use_global_device_ids=true | all-gather | bytes 1024000 | tf_op jit(solution)/shard_map/all_gather | solution.py:87
  115.9 6.1 copy.80
  122.0 0.2 fusion.2
  122.2 0.6 multiply_multiply_fusion.6
  122.8 1.0 fusion.4
  123.8 0.0 slice-start
  123.8 5.6 fusion.112
  129.5 0.9 copy-done
  130.4 7.0 %fusion = bf16[3200,1600]{0,1:T(8,128)(2,1)} fusion(bf16[128,3200]{1,0:T(8,128)(2,1)S(1)} %bitcast.27, f32[128,1600]{0,1:T(8,128)S(1)} %fusion.112), kind=kOutput, calls=%fused_computation.3 | convolution fusion | flops 1334272000 | bytes 11878400 | tf_op jit(solution)/shard_map/dot_general | solution.py:127
  137.4 4.2 fusion.1
  141.6 1.7 convolution_convert_fusion
  143.4 5.3 multiply_convert_fusion.1
  148.7 5.6 copy.89
  154.3 8.2 %reshape.40 = bf16[3200,128]{1,0:T(8,128)(2,1)} reshape(bf16[3200,8,16]{2,1,0:T(8,128)(2,1)} %bitcast.21) | data formatting | bytes 1638400
  162.5 0.0 reduce-scatter.5.cloned.1.call-update
  162.5 0.3 all-reduce.4.cloned.1.call-start
  162.8 21.7 %pad_maximum_fusion = bf16[3200,3200]{0,1:T(8,128)(2,1)} fusion(bf16[3200,1600]{0,1:T(8,128)(2,1)} %fusion, bf16[3200,1600]{0,1:T(8,128)(2,1)} %multiply_convert_fusion.1), kind=kLoop, calls=%fused_computation | loop fusion | flops 40960000 | bytes 40960000 | tf_op jit(solution)/shard_map/concatenate | solution.py:121
  184.5 0.0 all-reduce.4.cloned.1.call-update
  184.6 0.9 dynamic_slice.7
  185.5 0.6 dynamic-slice
  186.7 0.0 reduce-scatter.5.cloned.1.call-done
  186.7 2.1 reshape.41
  188.9 1.9 copy.90
  190.7 0.2 fusion.27
  190.9 6.2 psum.21
  197.1 0.7 fusion.37
  197.8 1.3 collective-permute-start.5
  199.1 4.6 collective-permute-start.4
  203.8 0.1 stack.39
  203.9 213.0 %collective-permute-done.4 = bf16[1,16,800]{2,1,0:T(8,128)(2,1)S(1)} collective-permute-done((bf16[1,16,800]{2,1,0:T(8,128)(2,1)S(1)}, bf16[1,16,800]{2,1,0:T(8,128)(2,1)S(1)}, u32[]{:S(2)}, u32[]{:S(2)}) %collective-permute-start.4) | collective-permute-done | bytes 25632 | tf_op jit(solution)/shard_map/ppermute | solution.py:17
  416.9 0.1 pad_maximum_fusion.3
  417.0 1.3 collective-permute-start.7
  418.3 4.5 collective-permute-start.6
  422.8 177.0 %all-reduce.1 = (f32[3,3,800]{2,1,0:T(4,128)}, f32[800]{0:T(1024)}) all-reduce(f32[3,3,800]{2,1,0:T(4,128)S(1)} %mul.381, f32[800]{0:T(1024)S(1)} %broadcast_multiply_fusion.1), channel_id=1, replica_groups=mesh['row'=4,'col'=8,'tp'=4] {'row','col'}, use_global_device_ids=true, to_apply=%region_14.0 | all-reduce | flops 8000 | bytes 64000 | tf_op jit(solution)/shard_map/psum | solution.py:147
  599.9 0.2 maximum_convert_fusion.1
  600.2 1.1 fusion.28
  601.2 60.7 %all-reduce.4.cloned.1.call-done = bf16[3200,3200]{0,1:T(8,128)(2,1)} async-done(((bf16[3200,3200]{0,1:T(8,128)(2,1)}), bf16[3200,3200]{0,1:T(8,128)(2,1)}) %all-reduce.4.cloned.1.call-update) | async-done | bytes 20480016
  661.9 1.7 dynamic-slice_convert_fusion
  663.7 0.1 fusion.108
  663.8 1.2 copy.87
  664.9 1.2 copy.88
  (76 shorter events, 0.4 us)
Async XLA Ops:
  8.0 64.7 %copy-start.1 = (bf16[8,16,800]{2,1,0:T(8,128)(2,1)S(1)}, bf16[8,16,800]{2,1,0:T(8,128)(2,1)}, u32[]{:S(2)}) copy-start(bf16[8,16,800]{2,1,0:T(8,128)(2,1)} %param.6) | copy-start | bytes 614404
  8.0 178.7 %reduce-scatter.5.cloned.1.call-start = ((), (), s32[]{:S(2)}) async-start(), calls=%async_computation.1 | async-start | bytes 1024000
  8.9 8.1 %collective-permute-start = (bf16[1,16,800]{2,1,0:T(8,128)(2,1)S(1)}, bf16[1,16,800]{2,1,0:T(8,128)(2,1)S(1)}, u32[]{:S(2)}, u32[]{:S(2)}) collective-permute-start(bf16[1,16,800]{2,1,0:T(8,128)(2,1)S(1)} %get-tuple-element.67), channel_id=1, source_target_pairs={{0,32},{32,64},{64,96},{1,33},{33,65},{65,97},{2,34},{34,66},{66,9... | collective-permute-start | bytes 76808 | tf_op jit(solution)/shard_map/ppermute | solution.py:17
  12.8 5.8 collective-permute-start.1
  18.6 53.5 %collective-permute-start.3 = (bf16[10,1,800]{2,0,1:T(8,128)(2,1)S(1)}, bf16[10,1,800]{2,0,1:T(8,128)(2,1)S(1)}, u32[]{:S(2)}, u32[]{:S(2)}) collective-permute-start(bf16[10,1,800]{2,0,1:T(8,128)(2,1)S(1)} %copy.94), channel_id=1, source_target_pairs={{4,0},{8,4},{12,8},{16,12},{20,16},{24,20},{28,24},{5,1},{9,5},{13... | collective-permute-start | bytes 48008 | tf_op jit(solution)/shard_map/ppermute | solution.py:19
  19.9 52.2 %collective-permute-start.2 = (bf16[10,1,800]{2,0,1:T(8,128)(2,1)S(1)}, bf16[10,1,800]{2,0,1:T(8,128)(2,1)S(1)}, u32[]{:S(2)}, u32[]{:S(2)}) collective-permute-start(bf16[10,1,800]{2,0,1:T(8,128)(2,1)S(1)} %copy.93), channel_id=1, source_target_pairs={{0,4},{4,8},{8,12},{12,16},{16,20},{20,24},{24,28},{1,5},{5,9},{9,... | collective-permute-start | bytes 48008 | tf_op jit(solution)/shard_map/ppermute | solution.py:17
  72.1 0.6 copy-start.5
  72.1 0.6 copy-start.7
  72.1 0.6 copy-start.9
  72.1 0.6 copy-start.11
  72.1 0.6 copy-start.13
  72.1 0.6 copy-start.15
  72.1 0.6 copy-start.17
  72.1 49.9 %copy-start.3 = (f32[800]{0:T(1024)}, f32[800]{0:T(1024)S(1)}, u32[]{:S(2)}) copy-start(f32[800]{0:T(1024)S(1)} %get-tuple-element.47) | copy-start | bytes 9604
  123.8 13.6 %slice-start.3 = ((s8[10240000]{0:T(1024)(128)(4,1)}), s8[4194304]{0:T(1024)(128)(4,1)S(1)}, s32[]{:S(2)}) async-start(s8[10240000]{0:T(1024)(128)(4,1)} %bitcast.22), calls=%async_computation.6 | async-start | bytes 8388608
  123.8 17.8 %slice-start = ((s8[10240000]{0:T(1024)(128)(4,1)}), s8[4194304]{0:T(1024)(128)(4,1)S(1)}, s32[]{:S(2)}) async-start(s8[10240000]{0:T(1024)(128)(4,1)} %bitcast.19), calls=%async_computation.3 | async-start | bytes 8388608
  129.5 0.9 copy-start
  130.4 7.0 %slice-start.4 = ((s8[10240000]{0:T(1024)(128)(4,1)}), s8[4194304]{0:T(1024)(128)(4,1)S(1)}, s32[]{:S(2)}) async-start(s8[10240000]{0:T(1024)(128)(4,1)} %bitcast.22), calls=%async_computation.7 | async-start | bytes 8388608
  130.4 7.0 %slice-start.5 = ((s8[10240000]{0:T(1024)(128)(4,1)}), s8[1851392]{0:T(1024)(128)(4,1)S(1)}, s32[]{:S(2)}) async-start(s8[10240000]{0:T(1024)(128)(4,1)} %bitcast.22), calls=%async_computation.8 | async-start | bytes 3702784
  130.4 11.2 %slice-start.1 = ((s8[10240000]{0:T(1024)(128)(4,1)}), s8[4194304]{0:T(1024)(128)(4,1)S(1)}, s32[]{:S(2)}) async-start(s8[10240000]{0:T(1024)(128)(4,1)} %bitcast.19), calls=%async_computation.4 | async-start | bytes 8388608
  130.4 11.2 %slice-start.2 = ((s8[10240000]{0:T(1024)(128)(4,1)}), s8[1851392]{0:T(1024)(128)(4,1)S(1)}, s32[]{:S(2)}) async-start(s8[10240000]{0:T(1024)(128)(4,1)} %bitcast.19), calls=%async_computation.5 | async-start | bytes 3702784
  162.5 499.4 %all-reduce.4.cloned.1.call-start = ((), (), s32[]{:S(2)}) async-start(), calls=%async_computation.2 | async-start | bytes 40960000
  184.5 1.0 copy-start.20
  184.5 12.6 %copy-start.2 = (bf16[8,16,800]{2,1,0:T(8,128)(2,1)S(1)}, bf16[8,16,800]{2,1,0:T(8,128)(2,1)}, u32[]{:S(2)}) copy-start(bf16[8,16,800]{2,1,0:T(8,128)(2,1)} %param.7) | copy-start | bytes 614404
  184.5 12.6 %copy-start.19 = (f32[8,16]{1,0:T(8,128)S(1)}, f32[8,16]{1,0:T(8,128)}, u32[]{:S(2)}) copy-start(f32[8,16]{1,0:T(8,128)} %get-tuple-element.68) | copy-start | bytes 1540
  184.5 415.6 %copy-start.4 = (f32[800]{0:T(1024)S(1)}, f32[800]{0:T(1024)}, u32[]{:S(2)}) copy-start(f32[800]{0:T(1024)} %copy-done.3) | copy-start | bytes 9604
  184.5 415.6 %copy-start.6 = (f32[800]{0:T(1024)S(1)}, f32[800]{0:T(1024)}, u32[]{:S(2)}) copy-start(f32[800]{0:T(1024)} %copy-done.5) | copy-start | bytes 9604
  184.6 415.6 %copy-start.8 = (f32[800]{0:T(1024)S(1)}, f32[800]{0:T(1024)}, u32[]{:S(2)}) copy-start(f32[800]{0:T(1024)} %copy-done.7) | copy-start | bytes 9604
  184.6 415.6 %copy-start.10 = (f32[800]{0:T(1024)S(1)}, f32[800]{0:T(1024)}, u32[]{:S(2)}) copy-start(f32[800]{0:T(1024)} %copy-done.9) | copy-start | bytes 9604
  184.6 415.6 %copy-start.12 = (f32[800]{0:T(1024)S(1)}, f32[800]{0:T(1024)}, u32[]{:S(2)}) copy-start(f32[800]{0:T(1024)} %copy-done.11) | copy-start | bytes 9604
  184.6 415.6 %copy-start.14 = (f32[800]{0:T(1024)S(1)}, f32[800]{0:T(1024)}, u32[]{:S(2)}) copy-start(f32[800]{0:T(1024)} %copy-done.13) | copy-start | bytes 9604
  184.6 415.6 %copy-start.16 = (f32[800]{0:T(1024)S(1)}, f32[800]{0:T(1024)}, u32[]{:S(2)}) copy-start(f32[800]{0:T(1024)} %copy-done.15) | copy-start | bytes 9604
  184.6 415.6 %copy-start.18 = (f32[800]{0:T(1024)S(1)}, f32[800]{0:T(1024)}, u32[]{:S(2)}) copy-start(f32[800]{0:T(1024)} %copy-done.17) | copy-start | bytes 9604
  197.8 6.1 collective-permute-start.5
  199.1 217.8 %collective-permute-start.4 = (bf16[1,16,800]{2,1,0:T(8,128)(2,1)S(1)}, bf16[1,16,800]{2,1,0:T(8,128)(2,1)S(1)}, u32[]{:S(2)}, u32[]{:S(2)}) collective-permute-start(bf16[1,16,800]{2,1,0:T(8,128)(2,1)S(1)} %get-tuple-element.64), channel_id=1, source_target_pairs={{0,32},{32,64},{64,96},{1,33},{33,65},{65,97},{2,34},{34,66},{66,9... | collective-permute-start | bytes 76808 | tf_op jit(solution)/shard_map/ppermute | solution.py:17
  417.0 182.9 %collective-permute-start.7 = (bf16[10,1,800]{2,0,1:T(8,128)(2,1)S(1)}, bf16[10,1,800]{2,0,1:T(8,128)(2,1)S(1)}, u32[]{:S(2)}, u32[]{:S(2)}) collective-permute-start(bf16[10,1,800]{2,0,1:T(8,128)(2,1)S(1)} %copy.84), channel_id=1, source_target_pairs={{4,0},{8,4},{12,8},{16,12},{20,16},{24,20},{28,24},{5,1},{9,5},{13... | collective-permute-start | bytes 48008 | tf_op jit(solution)/shard_map/ppermute | solution.py:19
  418.3 181.6 %collective-permute-start.6 = (bf16[10,1,800]{2,0,1:T(8,128)(2,1)S(1)}, bf16[10,1,800]{2,0,1:T(8,128)(2,1)S(1)}, u32[]{:S(2)}, u32[]{:S(2)}) collective-permute-start(bf16[10,1,800]{2,0,1:T(8,128)(2,1)S(1)} %copy.83), channel_id=1, source_target_pairs={{0,4},{4,8},{8,12},{12,16},{16,20},{20,24},{24,28},{1,5},{5,9},{9,... | collective-permute-start | bytes 48008 | tf_op jit(solution)/shard_map/ppermute | solution.py:17
Sparse Core Ops, SparseCore 0:
  162.6 22.7 reduce-scatter.4
Sparse Core Ops, SparseCore 1:
  184.6 477.3 all-reduce.3
where the time goes:
time: 675 us; the launch traced here: 674 us
  waiting for transfers between devices  274 us (41%)
  blocking collectives  264 us (39%)
  local copies, waits for them, and re-layouts  43.2 us (6%)
  other arithmetic  28 us (4%)
  matrix products  23.8 us (4%)
  starting transfers between devices  23 us (3%)
  between operations  16.8 us (2%)
    ppermute x4, waiting for transfers between devices, padded_2(): lax.ppermute(tail, axis, [(i, (i + 1) % count) for i in range(ends)])  213 us
    psum x1, blocking collectives, on_device(): lax.psum((local_gain, local_kernel), ('row', 'col'))  177 us
    unnamed x4, waiting for transfers between devices  60.8 us
    all_gather x1, blocking collectives, on_device(): lax.all_gather(own_h, 'tp', axis=2, tiled=True)  40.8 us
    all_gather x1, blocking collectives, on_device(): lax.all_gather(cotangent, 'tp', axis=2, tiled=True)  40.4 us
    unnamed x66, local copies, waits for them, and re-layouts  25.9 us
    concatenate x1, other arithmetic, on_device(): jnp.concatenate([lax.dot_general(normed, d_pre, (((0,), (0,)), ((), ())),...  21.7 us
    ppermute x4, starting transfers between devices, padded_2(): lax.ppermute(tail, axis, [(i, (i + 1) % count) for i in range(ends)])  17.6 us
  transfers between devices with their start and end apart: 10, of which 3 were waited for; matrix products, arithmetic and copies ran while one was open for 6% of the time, Pallas kernels for 0%

commit v1 on v0

--- a/solution.py
+++ b/solution.py
@@ -144,7 +144,7 @@
     local_kernel = (
         kernel_terms(dh_float, padded_x.astype(jnp.float32), row_cells, col_cells) * factor
     )
-    grad_gain, grad_kernel = lax.psum((local_gain, local_kernel), ("row", "col"))
+    grad_gain, grad_kernel = lax.psum(lax.psum((local_gain, local_kernel), "col"), "row")
     return (grad_tokens, grad_expand, grad_reduce, grad_kernel, grad_gain)
 
 

time: 675 us -> 673 us (level)
  waiting for transfers between devices: 274 us -> 229 us
  blocking collectives: 264 us -> 308 us
    ppermute x4, waiting for transfers between devices: 213 us -> 0.01 us  [padded_2(): lax.ppermute(tail, axis, [(i, (i + 1) % count) for i in range(ends)])]
    unnamed x4, waiting for transfers between devices: 60.8 us -> 228 us
    psum x1 -> x2, blocking collectives: 177 us -> 221 us  [the longest x1 179 us: on_device(): lax.psum(lax.psum((local_gain, local_kernel), 'col'), 'row')]
  transfers between devices with their start and end apart: 10 -> 10, of which waited for: 3 -> 2; matrix products, arithmetic and copies ran while one was open for 6% -> 6% of each run, Pallas kernels for 0% -> 0%
where the time goes in v1:
time: 673 us; the launch traced here: 672 us
  blocking collectives  308 us (46%)
  waiting for transfers between devices  229 us (34%)
  local copies, waits for them, and re-layouts  43.2 us (6%)
  other arithmetic  28 us (4%)
  matrix products  23.8 us (4%)
  starting transfers between devices  23 us (3%)
  between operations  16.8 us (2%)
    unnamed x4, waiting for transfers between devices  228 us
    psum x1, blocking collectives, on_device(): lax.psum(lax.psum((local_gain, local_kernel), 'col'), 'row')  179 us
    psum x1, blocking collectives, on_device(): lax.psum((local_gain, local_kernel), 'col')  42.4 us
    all_gather x1, blocking collectives, on_device(): lax.all_gather(own_h, 'tp', axis=2, tiled=True)  40.8 us
    all_gather x1, blocking collectives, on_device(): lax.all_gather(cotangent, 'tp', axis=2, tiled=True)  40.4 us
    unnamed x66, local copies, waits for them, and re-layouts  25.9 us
    concatenate x1, other arithmetic, on_device(): jnp.concatenate([lax.dot_general(normed, d_pre, (((0,), (0,)), ((), ())),...  21.7 us
    ppermute x4, starting transfers between devices, padded_2(): lax.ppermute(tail, axis, [(i, (i + 1) % count) for i in range(ends)])  17.6 us
  transfers between devices with their start and end apart: 10, of which 2 were waited for; matrix products, arithmetic and copies ran while one was open for 6% of the time, Pallas kernels for 0%

profile of v1, /device:TPU:0, one launch (start us, length us, event | category | flops | bytes accessed | tf_op | source)
XLA Modules:
  0.0 671.9 jit_solution(5208652539062995992)
XLA Ops:
  8.0 0.0 reduce-scatter.5.cloned.1.call-start
  8.1 0.8 fusion.111
  8.9 3.9 collective-permute-start
  12.8 1.3 collective-permute-start.1
  14.1 2.9 copy.81
  17.0 1.0 constant_dynamic-update-slice_fusion.1
  17.9 0.6 collective-permute-done.1
  18.6 0.1 fusion.109
  18.6 1.3 collective-permute-start.3
  19.9 4.5 collective-permute-start.2
  24.5 40.4 %all_gather.7 = bf16[8,16,3200]{1,0,2:T(8,128)(2,1)} all-gather(bf16[8,16,800]{1,0,2:T(8,128)(2,1)S(1)} %copy.81), channel_id=1, replica_groups=mesh['row'=4,'col'=8,'tp'=4] {'tp'}, dimensions={2}, use_global_device_ids=true | all-gather | bytes 1024000 | tf_op jit(solution)/shard_map/all_gather | solution.py:88
  64.9 6.1 copy.82
  71.0 1.0 dynamic-slice_reduce_fusion.8
  72.2 0.2 maximum_convert_fusion
  72.4 0.2 copy-done.5
  72.6 0.0 copy-done.7
  72.7 0.0 copy-done.9
  72.7 0.0 copy-done.11
  72.7 0.0 copy-done.13
  72.7 0.0 copy-done.15
  72.7 0.0 copy-done.17
  72.7 0.4 add_convert_fusion
  73.1 2.0 copy.79
  75.1 40.8 %all_gather.6 = bf16[8,16,3200]{1,0,2:T(8,128)(2,1)} all-gather(bf16[8,16,800]{1,0,2:T(8,128)(2,1)S(1)} %copy.79), channel_id=1, replica_groups=mesh['row'=4,'col'=8,'tp'=4] {'tp'}, dimensions={2}, use_global_device_ids=true | all-gather | bytes 1024000 | tf_op jit(solution)/shard_map/all_gather | solution.py:87
  115.9 6.1 copy.80
  122.0 0.2 fusion.2
  122.2 0.6 multiply_multiply_fusion.6
  122.8 1.0 fusion.4
  123.8 0.0 slice-start
  123.8 5.6 fusion.112
  129.5 0.9 copy-done
  130.4 7.0 %fusion = bf16[3200,1600]{0,1:T(8,128)(2,1)} fusion(bf16[128,3200]{1,0:T(8,128)(2,1)S(1)} %bitcast.27, f32[128,1600]{0,1:T(8,128)S(1)} %fusion.112), kind=kOutput, calls=%fused_computation.3 | convolution fusion | flops 1334272000 | bytes 11878400 | tf_op jit(solution)/shard_map/dot_general | solution.py:127
  137.4 4.2 fusion.1
  141.6 1.7 convolution_convert_fusion
  143.4 5.3 multiply_convert_fusion.1
  148.7 5.6 copy.89
  154.3 8.2 %reshape.40 = bf16[3200,128]{1,0:T(8,128)(2,1)} reshape(bf16[3200,8,16]{2,1,0:T(8,128)(2,1)} %bitcast.21) | data formatting | bytes 1638400
  162.5 0.0 reduce-scatter.5.cloned.1.call-update
  162.5 0.3 all-reduce.5.cloned.1.call-start
  162.8 21.7 %pad_maximum_fusion = bf16[3200,3200]{0,1:T(8,128)(2,1)} fusion(bf16[3200,1600]{0,1:T(8,128)(2,1)} %fusion, bf16[3200,1600]{0,1:T(8,128)(2,1)} %multiply_convert_fusion.1), kind=kLoop, calls=%fused_computation | loop fusion | flops 40960000 | bytes 40960000 | tf_op jit(solution)/shard_map/concatenate | solution.py:121
  184.5 0.0 all-reduce.5.cloned.1.call-update
  184.6 0.9 dynamic_slice.7
  185.5 0.6 dynamic-slice
  186.7 0.0 reduce-scatter.5.cloned.1.call-done
  186.7 2.1 reshape.41
  188.9 1.9 copy.90
  190.7 0.2 fusion.27
  190.9 6.2 psum.35
  197.1 0.7 fusion.37
  197.8 1.3 collective-permute-start.5
  199.1 4.6 collective-permute-start.4
  203.8 0.1 stack.39
  203.9 42.4 %all-reduce.1 = (f32[3,3,800]{2,1,0:T(4,128)S(1)}, f32[800]{0:T(1024)S(1)}) all-reduce(f32[3,3,800]{2,1,0:T(4,128)S(1)} %mul.381, f32[800]{0:T(1024)S(1)} %broadcast_multiply_fusion.1), channel_id=1, replica_groups=mesh['row'=4,'col'=8,'tp'=4] {'col'}, use_global_device_ids=true, to_apply=%region_14.0 | all-reduce | flops 8000 | bytes 64000 | tf_op jit(solution)/shard_map/psum | solution.py:147
  246.4 0.1 pad_maximum_fusion.3
  246.5 1.3 collective-permute-start.7
  247.8 4.5 collective-permute-start.6
  252.3 178.5 %all-reduce.2 = (f32[3,3,800]{2,1,0:T(4,128)}, f32[800]{0:T(1024)}) all-reduce(f32[3,3,800]{2,1,0:T(4,128)S(1)} %get-tuple-element.55, f32[800]{0:T(1024)S(1)} %get-tuple-element.56), channel_id=1, replica_groups=mesh['row'=4,'col'=8,'tp'=4] {'row'}, use_global_device_ids=true, to_apply=%region_15.0 | all-reduce | flops 8000 | bytes 64000 | tf_op jit(solution)/shard_map/psum | solution.py:147
  430.9 0.2 maximum_convert_fusion.1
  431.2 1.1 fusion.28
  432.2 228.1 %all-reduce.5.cloned.1.call-done = bf16[3200,3200]{0,1:T(8,128)(2,1)} async-done(((bf16[3200,3200]{0,1:T(8,128)(2,1)}), bf16[3200,3200]{0,1:T(8,128)(2,1)}) %all-reduce.5.cloned.1.call-update) | async-done | bytes 20480016
  660.3 1.7 dynamic-slice_convert_fusion
  662.0 0.1 fusion.108
  662.2 1.2 copy.87
  663.3 1.2 copy.88
  (77 shorter events, 0.4 us)
Async XLA Ops:
  8.0 64.7 %copy-start.1 = (bf16[8,16,800]{2,1,0:T(8,128)(2,1)S(1)}, bf16[8,16,800]{2,1,0:T(8,128)(2,1)}, u32[]{:S(2)}) copy-start(bf16[8,16,800]{2,1,0:T(8,128)(2,1)} %param.6) | copy-start | bytes 614404
  8.0 178.7 %reduce-scatter.5.cloned.1.call-start = ((), (), s32[]{:S(2)}) async-start(), calls=%async_computation.1 | async-start | bytes 1024000
  8.9 8.1 %collective-permute-start = (bf16[1,16,800]{2,1,0:T(8,128)(2,1)S(1)}, bf16[1,16,800]{2,1,0:T(8,128)(2,1)S(1)}, u32[]{:S(2)}, u32[]{:S(2)}) collective-permute-start(bf16[1,16,800]{2,1,0:T(8,128)(2,1)S(1)} %get-tuple-element.69), channel_id=1, source_target_pairs={{0,32},{32,64},{64,96},{1,33},{33,65},{65,97},{2,34},{34,66},{66,9... | collective-permute-start | bytes 76808 | tf_op jit(solution)/shard_map/ppermute | solution.py:17
  12.8 5.8 collective-permute-start.1
  18.6 53.5 %collective-permute-start.3 = (bf16[10,1,800]{2,0,1:T(8,128)(2,1)S(1)}, bf16[10,1,800]{2,0,1:T(8,128)(2,1)S(1)}, u32[]{:S(2)}, u32[]{:S(2)}) collective-permute-start(bf16[10,1,800]{2,0,1:T(8,128)(2,1)S(1)} %copy.94), channel_id=1, source_target_pairs={{4,0},{8,4},{12,8},{16,12},{20,16},{24,20},{28,24},{5,1},{9,5},{13... | collective-permute-start | bytes 48008 | tf_op jit(solution)/shard_map/ppermute | solution.py:19
  19.9 52.2 %collective-permute-start.2 = (bf16[10,1,800]{2,0,1:T(8,128)(2,1)S(1)}, bf16[10,1,800]{2,0,1:T(8,128)(2,1)S(1)}, u32[]{:S(2)}, u32[]{:S(2)}) collective-permute-start(bf16[10,1,800]{2,0,1:T(8,128)(2,1)S(1)} %copy.93), channel_id=1, source_target_pairs={{0,4},{4,8},{8,12},{12,16},{16,20},{20,24},{24,28},{1,5},{5,9},{9,... | collective-permute-start | bytes 48008 | tf_op jit(solution)/shard_map/ppermute | solution.py:17
  72.1 0.6 copy-start.5
  72.1 0.6 copy-start.7
  72.1 0.6 copy-start.9
  72.1 0.6 copy-start.11
  72.1 0.6 copy-start.13
  72.1 0.6 copy-start.15
  72.1 0.6 copy-start.17
  72.1 49.9 %copy-start.3 = (f32[800]{0:T(1024)}, f32[800]{0:T(1024)S(1)}, u32[]{:S(2)}) copy-start(f32[800]{0:T(1024)S(1)} %get-tuple-element.47) | copy-start | bytes 9604
  123.8 13.6 %slice-start.3 = ((s8[10240000]{0:T(1024)(128)(4,1)}), s8[4194304]{0:T(1024)(128)(4,1)S(1)}, s32[]{:S(2)}) async-start(s8[10240000]{0:T(1024)(128)(4,1)} %bitcast.22), calls=%async_computation.6 | async-start | bytes 8388608
  123.8 17.8 %slice-start = ((s8[10240000]{0:T(1024)(128)(4,1)}), s8[4194304]{0:T(1024)(128)(4,1)S(1)}, s32[]{:S(2)}) async-start(s8[10240000]{0:T(1024)(128)(4,1)} %bitcast.19), calls=%async_computation.3 | async-start | bytes 8388608
  129.5 0.9 copy-start
  130.4 7.0 %slice-start.4 = ((s8[10240000]{0:T(1024)(128)(4,1)}), s8[4194304]{0:T(1024)(128)(4,1)S(1)}, s32[]{:S(2)}) async-start(s8[10240000]{0:T(1024)(128)(4,1)} %bitcast.22), calls=%async_computation.7 | async-start | bytes 8388608
  130.4 7.0 %slice-start.5 = ((s8[10240000]{0:T(1024)(128)(4,1)}), s8[1851392]{0:T(1024)(128)(4,1)S(1)}, s32[]{:S(2)}) async-start(s8[10240000]{0:T(1024)(128)(4,1)} %bitcast.22), calls=%async_computation.8 | async-start | bytes 3702784
  130.4 11.2 %slice-start.1 = ((s8[10240000]{0:T(1024)(128)(4,1)}), s8[4194304]{0:T(1024)(128)(4,1)S(1)}, s32[]{:S(2)}) async-start(s8[10240000]{0:T(1024)(128)(4,1)} %bitcast.19), calls=%async_computation.4 | async-start | bytes 8388608
  130.4 11.2 %slice-start.2 = ((s8[10240000]{0:T(1024)(128)(4,1)}), s8[1851392]{0:T(1024)(128)(4,1)S(1)}, s32[]{:S(2)}) async-start(s8[10240000]{0:T(1024)(128)(4,1)} %bitcast.19), calls=%async_computation.5 | async-start | bytes 3702784
  162.5 497.8 %all-reduce.5.cloned.1.call-start = ((), (), s32[]{:S(2)}) async-start(), calls=%async_computation.2 | async-start | bytes 40960000
  184.5 1.0 copy-start.20
  184.5 12.6 %copy-start.2 = (bf16[8,16,800]{2,1,0:T(8,128)(2,1)S(1)}, bf16[8,16,800]{2,1,0:T(8,128)(2,1)}, u32[]{:S(2)}) copy-start(bf16[8,16,800]{2,1,0:T(8,128)(2,1)} %param.7) | copy-start | bytes 614404
  184.5 12.6 %copy-start.19 = (f32[8,16]{1,0:T(8,128)S(1)}, f32[8,16]{1,0:T(8,128)}, u32[]{:S(2)}) copy-start(f32[8,16]{1,0:T(8,128)} %get-tuple-element.70) | copy-start | bytes 1540
  184.5 246.6 %copy-start.4 = (f32[800]{0:T(1024)S(1)}, f32[800]{0:T(1024)}, u32[]{:S(2)}) copy-start(f32[800]{0:T(1024)} %copy-done.3) | copy-start | bytes 9604
  184.5 246.6 %copy-start.6 = (f32[800]{0:T(1024)S(1)}, f32[800]{0:T(1024)}, u32[]{:S(2)}) copy-start(f32[800]{0:T(1024)} %copy-done.5) | copy-start | bytes 9604
  184.6 246.6 %copy-start.8 = (f32[800]{0:T(1024)S(1)}, f32[800]{0:T(1024)}, u32[]{:S(2)}) copy-start(f32[800]{0:T(1024)} %copy-done.7) | copy-start | bytes 9604
  184.6 246.6 %copy-start.10 = (f32[800]{0:T(1024)S(1)}, f32[800]{0:T(1024)}, u32[]{:S(2)}) copy-start(f32[800]{0:T(1024)} %copy-done.9) | copy-start | bytes 9604
  184.6 246.6 %copy-start.12 = (f32[800]{0:T(1024)S(1)}, f32[800]{0:T(1024)}, u32[]{:S(2)}) copy-start(f32[800]{0:T(1024)} %copy-done.11) | copy-start | bytes 9604
  184.6 246.6 %copy-start.14 = (f32[800]{0:T(1024)S(1)}, f32[800]{0:T(1024)}, u32[]{:S(2)}) copy-start(f32[800]{0:T(1024)} %copy-done.13) | copy-start | bytes 9604
  184.6 246.6 %copy-start.16 = (f32[800]{0:T(1024)S(1)}, f32[800]{0:T(1024)}, u32[]{:S(2)}) copy-start(f32[800]{0:T(1024)} %copy-done.15) | copy-start | bytes 9604
  184.6 246.6 %copy-start.18 = (f32[800]{0:T(1024)S(1)}, f32[800]{0:T(1024)}, u32[]{:S(2)}) copy-start(f32[800]{0:T(1024)} %copy-done.17) | copy-start | bytes 9604
  197.8 48.6 %collective-permute-start.5 = (bf16[1,16,800]{2,1,0:T(8,128)(2,1)S(1)}, bf16[1,16,800]{2,1,0:T(8,128)(2,1)S(1)}, u32[]{:S(2)}, u32[]{:S(2)}) collective-permute-start(bf16[1,16,800]{2,1,0:T(8,128)(2,1)S(1)} %get-tuple-element.67), channel_id=1, source_target_pairs={{32,0},{64,32},{96,64},{33,1},{65,33},{97,65},{34,2},{66,34},{98,6... | collective-permute-start | bytes 76808 | tf_op jit(solution)/shard_map/ppermute | solution.py:19
  199.1 47.3 %collective-permute-start.4 = (bf16[1,16,800]{2,1,0:T(8,128)(2,1)S(1)}, bf16[1,16,800]{2,1,0:T(8,128)(2,1)S(1)}, u32[]{:S(2)}, u32[]{:S(2)}) collective-permute-start(bf16[1,16,800]{2,1,0:T(8,128)(2,1)S(1)} %get-tuple-element.66), channel_id=1, source_target_pairs={{0,32},{32,64},{64,96},{1,33},{33,65},{65,97},{2,34},{34,66},{66,9... | collective-permute-start | bytes 76808 | tf_op jit(solution)/shard_map/ppermute | solution.py:17
  246.5 184.4 %collective-permute-start.7 = (bf16[10,1,800]{2,0,1:T(8,128)(2,1)S(1)}, bf16[10,1,800]{2,0,1:T(8,128)(2,1)S(1)}, u32[]{:S(2)}, u32[]{:S(2)}) collective-permute-start(bf16[10,1,800]{2,0,1:T(8,128)(2,1)S(1)} %copy.84), channel_id=1, source_target_pairs={{4,0},{8,4},{12,8},{16,12},{20,16},{24,20},{28,24},{5,1},{9,5},{13... | collective-permute-start | bytes 48008 | tf_op jit(solution)/shard_map/ppermute | solution.py:19
  247.8 183.1 %collective-permute-start.6 = (bf16[10,1,800]{2,0,1:T(8,128)(2,1)S(1)}, bf16[10,1,800]{2,0,1:T(8,128)(2,1)S(1)}, u32[]{:S(2)}, u32[]{:S(2)}) collective-permute-start(bf16[10,1,800]{2,0,1:T(8,128)(2,1)S(1)} %copy.83), channel_id=1, source_target_pairs={{0,4},{4,8},{8,12},{12,16},{16,20},{20,24},{24,28},{1,5},{5,9},{9,... | collective-permute-start | bytes 48008 | tf_op jit(solution)/shard_map/ppermute | solution.py:17
Sparse Core Ops, SparseCore 0:
  162.6 22.7 reduce-scatter.4
Sparse Core Ops, SparseCore 1:
  184.6 475.6 all-reduce.4
